TPU v7x, 32 devices: a whole 2x2x4 slice. The times are simulated.
32 devices in a mesh: row: 8 (over z, core), col: 4 (over y, x).
Axes of the slice: x: 2, y: 2, z: 4, core: 2. Of those that a mesh axis runs over, the one named last changes fastest.
Arguments:
- covariance: float32 [1, 8192, 8192], P(None, 'row', 'col'), may hold values from -120 to 120, as said below
- latitude_offset: int32 [1, 1, 8192], replicated, may hold values from -2 to 2
- longitude_offset: int32 [1, 1, 8192], replicated, may hold values from -3 to 3
- upwind: int32 [1, 1, 8192], replicated, may hold values from 0 to 3
- courant: float32 [1, 1, 8192], replicated, may hold values from 0.05 to 0.45
- longitude_diffusion: float32 [1, 8192], replicated, may hold values from 0.01 to 0.08
- latitude_diffusion: float32 [1, 8192], replicated, may hold values from 0.01 to 0.08
Outputs:
- forecast_cov: float32 [1, 8192, 8192], P(None, 'row', 'col')
Inputs may be any that keep to these rules, and one draw needn't show every extreme that they name: `covariance`: each level's matrix is symmetric up to rounding.
All inputs are finite; a program needn't handle non-finite values.
Results may differ from a plain program's by a relative error of at most 0.0003.
Values sent between devices are 32-bit elements; how exact they have to be, the bound alone decides.
A program may use at most 128 MiB of HBM per device.

v0:
```python
import jax
import jax.numpy as jnp
from jax import lax
from jax.sharding import PartitionSpec as P

NLAT = 64
NLON = 128


def predicted_covariance(
    field_stack,
    latitude_offset,
    longitude_offset,
    upwind,
    courant,
    longitude_diffusion,
    latitude_diffusion,
):
    cell_index = jnp.arange(NLAT * NLON, dtype=jnp.int32)
    lat_cell = cell_index // NLON
    lon_cell = cell_index % NLON
    lon_coeff = longitude_diffusion.reshape(NLAT, NLON)
    lat_coeff = latitude_diffusion.reshape(NLAT, NLON)
    cells_total = NLAT * NLON
    lat_depart = jnp.clip(lat_cell + latitude_offset[0], 0, NLAT - 1)
    lon_depart = (lon_cell + longitude_offset[0]) % NLON
    up_code = upwind[0]
    lat_near = jnp.clip(
        lat_depart + (up_code == 2).astype(jnp.int32) - (up_code == 3).astype(jnp.int32),
        0,
        NLAT - 1,
    )
    lon_near = (
        lon_depart + (up_code == 0).astype(jnp.int32) - (up_code == 1).astype(jnp.int32)
    ) % NLON
    depart = lat_depart * NLON + lon_depart
    near = lat_near * NLON + lon_near
    both_index = jnp.concatenate([depart, near])
    picked = jnp.take(field_stack, both_index, axis=1)
    weight = courant[0]
    shifted = (1.0 - weight) * picked[:, :cells_total] + weight * picked[:, cells_total:]
    grid_view = shifted.reshape(shifted.shape[0], NLAT, NLON)
    east_side = jnp.roll(grid_view, -1, axis=2)
    west_side = jnp.roll(grid_view, 1, axis=2)
    north_side = jnp.concatenate([grid_view[:, 1:], grid_view[:, -1:]], axis=1)
    south_side = jnp.concatenate([grid_view[:, :1], grid_view[:, :-1]], axis=1)
    grid_view = (
        grid_view
        + lon_coeff * (east_side + west_side - 2.0 * grid_view)
        + lat_coeff * (north_side + south_side - 2.0 * grid_view)
    )
    field_stack = grid_view.reshape(shifted.shape[0], NLAT * NLON)
    return field_stack


def body(
    covariance,
    latitude_offset,
    longitude_offset,
    upwind,
    courant,
    longitude_diffusion,
    latitude_diffusion,
):
    levels, block_rows, block_cols = covariance.shape
    col_count = lax.axis_size("col")
    row_count = lax.axis_size("row")
    devices_all = row_count * col_count
    field_rows = block_rows // col_count
    cells = block_cols * col_count

    def advance(packed):
        level_count, single, item_count, width_cells = packed.shape
        final_output = jax.vmap(predicted_covariance)(
            packed.reshape(level_count, item_count, width_cells),
            latitude_offset,
            longitude_offset,
            upwind,
            courant,
            longitude_diffusion,
            latitude_diffusion,
        )
        return final_output.reshape(level_count, single, item_count, width_cells)

    split_tiles = covariance.reshape(levels, col_count, field_rows, block_cols)
    row_fields = advance(
        lax.all_to_all(split_tiles, "col", split_axis=1, concat_axis=3, tiled=True)
    )
    row_fields = row_fields.reshape(levels, field_rows, cells)
    outgoing = jnp.transpose(
        row_fields.reshape(levels, field_rows, devices_all, field_rows), (0, 2, 3, 1)
    )
    turned = advance(
        lax.all_to_all(outgoing, ("row", "col"), split_axis=1, concat_axis=3, tiled=True)
    )
    turned = turned.reshape(levels, field_rows, cells)
    back_rows = turned.reshape(levels, field_rows, col_count, block_cols)
    regrouped = lax.all_to_all(back_rows, "col", split_axis=2, concat_axis=1, tiled=True)
    return regrouped.reshape(levels, block_rows, block_cols)


def solution(mesh):
    in_specs = (P(None, "row", "col"), P(), P(), P(), P(), P(), P())
    out_specs = P(None, "row", "col")
    return jax.shard_map(body, mesh=mesh, in_specs=in_specs, out_specs=out_specs, check_vma=False)
```

profile of v0, /device:TPU:1, one launch (start us, length us, event | category | flops | bytes accessed | tf_op | source)
XLA Modules:
  0.0 1022.4 jit_solution(5693209810478718411)
XLA Ops:
  0.0 8.7 copy.19
  8.7 5.8 all-to-all-start
  17.6 89.5 %all-to-all-done = f32[1,4,256,2048]{2,3,0,1:T(8,128)} async-done(((f32[1,4,256,2048]{2,3,0,1:T(8,128)}), f32[1,4,256,2048]{2,3,0,1:T(8,128)}, u32[]{:S(2)}, u32[]{:S(2)}) %all-to-all-start) | async-done | bytes 8388640 | tf_op jit(solution)/shard_map/all_to_all | solution.py:87
  107.1 247.5 %gather_fusion = f32[16384,256]{1,0:T(8,128)} fusion(f32[1,256,8192]{1,2,0:T(8,128)} %bitcast.10, s32[16384]{0:T(1024)S(1)} %bitcast.79), kind=kCustom, calls=%fused_computation.clone | custom fusion | bytes 33685504 | tf_op jit(solution)/shard_map/vmap(jit(_take))/gather | solution.py:39
  354.7 9.8 bitcast_select_fusion.1
  364.5 2.8 fusion.1
  367.3 6.7 fusion.25
  374.1 6.3 fusion.27
  380.4 6.6 maximum_add_fusion
  387.0 6.7 maximum_add_fusion.1
  393.7 4.7 add_bitcast_fusion
  398.4 6.2 all-to-all-start.1
  404.6 187.6 %all-to-all-done.1 = f32[1,32,256,256]{3,2,0,1:T(8,128)} async-done(((f32[1,32,256,256]{3,2,0,1:T(8,128)}), f32[1,32,256,256]{3,2,0,1:T(8,128)}, u32[]{:S(2)}, u32[]{:S(2)}) %all-to-all-start.1) | async-done | bytes 8388640 | tf_op jit(solution)/shard_map/all_to_all | solution.py:94
  592.2 8.9 copy.22
  601.2 261.8 %gather_fusion.1 = f32[16384,256]{1,0:T(8,128)} fusion(f32[1,256,8192]{1,2,0:T(8,128)} %bitcast.81, s32[16384]{0:T(1024)S(1)} %bitcast.80), kind=kCustom, calls=%fused_computation.1.clone | custom fusion | bytes 33685504 | tf_op jit(solution)/shard_map/vmap(jit(_take))/gather | solution.py:39
  863.0 9.8 bitcast_select_fusion
  872.9 2.8 fusion
  875.6 6.7 fusion.21
  882.5 6.3 fusion.23
  888.8 6.6 maximum_add_fusion.2
  895.4 9.5 maximum_add_fusion.3
  904.9 9.8 multiply_add_fusion
  914.6 99.1 %all_to_all.45 = f32[1,256,4,2048]{1,3,0,2:T(8,128)} all-to-all(f32[1,256,4,2048]{1,3,0,2:T(8,128)} %multiply_add_fusion), channel_id=1, replica_groups=mesh['row'=8,'col'=4] {'col'}, dimensions={2} | all-to-all | bytes 16777216 | tf_op jit(solution)/shard_map/all_to_all | solution.py:98
  1013.7 8.7 copy.25
  (29 shorter events, 3.3 us)
Async XLA Ops:
  8.7 5.8 copy-start.3
  8.7 5.8 copy-start.4
  8.7 6.0 copy-start.5
  8.7 6.3 copy-start
  8.7 6.9 copy-start.1
  8.7 7.6 copy-start.2
  8.7 98.4 %all-to-all-start = ((f32[1,4,256,2048]{2,3,0,1:T(8,128)}), f32[1,4,256,2048]{2,3,0,1:T(8,128)}, u32[]{:S(2)}, u32[]{:S(2)}) async-start(f32[1,4,256,2048]{2,3,0,1:T(8,128)} %copy.19), calls=%async_computation | async-start | bytes 16777216 | tf_op jit(solution)/shard_map/all_to_all | solution.py:87
  398.4 193.8 %all-to-all-start.1 = ((f32[1,32,256,256]{3,2,0,1:T(8,128)}), f32[1,32,256,256]{3,2,0,1:T(8,128)}, u32[]{:S(2)}, u32[]{:S(2)}) async-start(f32[1,32,256,256]{3,2,0,1:T(8,128)} %add_bitcast_fusion), calls=%async_computation.1 | async-start | bytes 16777216 | tf_op jit(solution)/shard_map/all_to_all | solution.py:94
where the time goes:
time: 1030 us; the launch traced here: 1020 us
  local copies, waits for them, and re-layouts  563 us (55%)
  waiting for transfers between devices  277 us (27%)
  blocking collectives  99.1 us (10%)
  other arithmetic  71.4 us (7%)
  starting transfers between devices  11.9 us (1%)
    gather x3, local copies, waits for them, and re-layouts, predicted_covariance(): picked = jnp.take(field_stack, both_index, axis=1)  509 us
    all_to_all x1, waiting for transfers between devices, body(): lax.all_to_all(outgoing, ('row', 'col'), split_axis=1, concat_axis=3, til...  188 us
    all_to_all x1, blocking collectives, body(): lax.all_to_all(back_rows, 'col', split_axis=2, concat_axis=1, tiled=True)  99.1 us
    all_to_all x1, waiting for transfers between devices, body(): lax.all_to_all(split_tiles, 'col', split_axis=1, concat_axis=3, tiled=True)  89.5 us
  transfers between devices with their start and end apart: 2, of which 2 were waited for; matrix products, arithmetic and copies ran while one was open for 0% of the time, Pallas kernels for 0%

commit v1 on v0

v1 whole, which is shorter than its diff:
```python
import functools

import jax
import jax.numpy as jnp
from jax import lax
from jax.experimental import pallas as pl
from jax.experimental.pallas import tpu as pltpu
from jax.sharding import PartitionSpec as P

NLAT = 64
NLON = 128
TAPS = 10
REACH = 4
HALO = REACH * NLON
PAIR = 2 * NLON
BAND = PAIR + 2 * HALO
EDGE = HALO
MIB = 1024 * 1024


def operator_taps(latitude_offset, longitude_offset, upwind, courant, longitude_diffusion, latitude_diffusion):
    cell = jnp.arange(NLAT * NLON, dtype=jnp.int32)
    lat_depart = jnp.clip(cell // NLON + latitude_offset, 0, NLAT - 1)
    lon_depart = (cell % NLON + longitude_offset) % NLON
    lat_near = jnp.clip(
        lat_depart + (upwind == 2).astype(jnp.int32) - (upwind == 3).astype(jnp.int32), 0, NLAT - 1
    )
    lon_near = (
        lon_depart + (upwind == 0).astype(jnp.int32) - (upwind == 1).astype(jnp.int32)
    ) % NLON
    depart = (lat_depart * NLON + lon_depart).reshape(NLAT, NLON)
    near = (lat_near * NLON + lon_near).reshape(NLAT, NLON)
    weight = courant.reshape(NLAT, NLON)
    lon_c = longitude_diffusion.reshape(NLAT, NLON)
    lat_c = latitude_diffusion.reshape(NLAT, NLON)

    def five(grid):
        return [
            grid,
            jnp.roll(grid, -1, axis=1),
            jnp.roll(grid, 1, axis=1),
            jnp.concatenate([grid[1:], grid[-1:]], axis=0),
            jnp.concatenate([grid[:1], grid[:-1]], axis=0),
        ]

    coeffs = [1.0 - 2.0 * lon_c - 2.0 * lat_c, lon_c, lon_c, lat_c, lat_c]
    far = [f * (1.0 - w) for f, w in zip(coeffs, five(weight))]
    close = [f * w for f, w in zip(coeffs, five(weight))]
    base = ((cell // PAIR) * PAIR - HALO).reshape(NLAT, NLON)
    source = jnp.stack([s - base for s in five(depart) + five(near)]).reshape(TAPS, -1)
    return source, jnp.stack(far + close).reshape(TAPS, -1)


def band_kernel(source_ref, weight_ref, high_ref, low_ref, *, turned):
    lon = lax.broadcasted_iota(jnp.int32, (NLON, PAIR), 0)
    for row in range(BAND // NLON):
        here = lon + row * NLON
        total = jnp.zeros((NLON, PAIR), jnp.float32)
        for tap in range(TAPS):
            total += jnp.where(here == source_ref[tap : tap + 1, :], weight_ref[tap : tap + 1, :], 0.0)
        if turned:
            total = total.T
        high = total.astype(jnp.bfloat16)
        low = (total - high.astype(jnp.float32)).astype(jnp.bfloat16)
        where = pl.ds(row * NLON, NLON)
        if turned:
            high_ref[0, :, where] = high
            low_ref[0, :, where] = low
        else:
            high_ref[0, where, :] = high
            low_ref[0, where, :] = low


def build_bands(source, weight, turned):
    pairs = source.shape[1] // PAIR
    shape = (PAIR, BAND) if turned else (BAND, PAIR)
    out = jax.ShapeDtypeStruct((pairs,) + shape, jnp.bfloat16)
    taps = pl.BlockSpec((TAPS, PAIR), lambda p: (0, p))
    block = pl.BlockSpec((1,) + shape, lambda p: (p, 0, 0))
    return pl.pallas_call(
        functools.partial(band_kernel, turned=turned),
        grid=(pairs,),
        in_specs=[taps, taps],
        out_specs=[block, block],
        out_shape=[out, out],
        compiler_params=pltpu.CompilerParams(vmem_limit_bytes=32 * MIB),
        cost_estimate=pl.CostEstimate(
            flops=pairs * BAND * PAIR * 3 * TAPS * 16, bytes_accessed=pairs * BAND * PAIR * 4, transcendentals=0
        ),
    )(source, weight)


def halves(x):
    high = x.astype(jnp.bfloat16)
    return high, (x - high.astype(jnp.float32)).astype(jnp.bfloat16)


def dot(a, b):
    return jnp.dot(a, b, preferred_element_type=jnp.float32)


def right_kernel(*refs, parts, pairs):
    x_refs, (high_ref, low_ref, out_ref) = refs[:parts], refs[parts:]
    split = [halves(r[...]) for r in x_refs]
    high = jnp.concatenate([s[0] for s in split], axis=1) if parts > 1 else split[0][0]
    low = jnp.concatenate([s[1] for s in split], axis=1) if parts > 1 else split[0][1]
    for p in range(pairs):
        xh = high[:, p * PAIR : p * PAIR + BAND]
        xl = low[:, p * PAIR : p * PAIR + BAND]
        out_ref[:, p * PAIR : (p + 1) * PAIR] = (
            dot(xh, low_ref[p]) + dot(xl, high_ref[p]) + dot(xh, high_ref[p])
        )


def apply_right(parts, high, low, first, pairs, tile=256):
    rows = parts[0][0].shape[0]
    tile = min(tile, rows)
    specs = [pl.BlockSpec((tile, w), lambda i, k=start // w: (i, k)) for _, start, w in parts]
    high, low = high[first : first + pairs], low[first : first + pairs]
    bands = pl.BlockSpec((pairs, BAND, PAIR), lambda i: (0, 0, 0))
    width = pairs * PAIR
    return pl.pallas_call(
        functools.partial(right_kernel, parts=len(parts), pairs=pairs),
        grid=(rows // tile,),
        in_specs=specs + [bands, bands],
        out_specs=pl.BlockSpec((tile, width), lambda i: (i, 0)),
        out_shape=jax.ShapeDtypeStruct((rows, width), jnp.float32),
        compiler_params=pltpu.CompilerParams(vmem_limit_bytes=48 * MIB),
        cost_estimate=pl.CostEstimate(
            flops=6 * rows * BAND * width, bytes_accessed=rows * width * 12, transcendentals=0
        ),
    )(*[p[0] for p in parts], high, low)


def left_kernel(up_ref, own_ref, down_ref, high_ref, low_ref, out_ref, *, pairs):
    split = [halves(r[...]) for r in (up_ref, own_ref, down_ref)]
    high = jnp.concatenate([s[0] for s in split], axis=0)
    low = jnp.concatenate([s[1] for s in split], axis=0)
    for q in range(pairs):
        xh = high[q * PAIR : q * PAIR + BAND]
        xl = low[q * PAIR : q * PAIR + BAND]
        out_ref[q * PAIR : (q + 1) * PAIR, :] = (
            dot(low_ref[q], xh) + dot(high_ref[q], xl) + dot(high_ref[q], xh)
        )


def apply_left(up, own, down, high, low, tile=256):
    rows, width = own.shape
    tile = min(tile, width)
    pairs = rows // PAIR
    column = lambda i: (0, i)
    bands = pl.BlockSpec((pairs, PAIR, BAND), lambda i: (0, 0, 0))
    return pl.pallas_call(
        functools.partial(left_kernel, pairs=pairs),
        grid=(width // tile,),
        in_specs=[
            pl.BlockSpec((HALO, tile), column),
            pl.BlockSpec((rows, tile), column),
            pl.BlockSpec((HALO, tile), column),
            bands,
            bands,
        ],
        out_specs=pl.BlockSpec((rows, tile), column),
        out_shape=jax.ShapeDtypeStruct((rows, width), jnp.float32),
        compiler_params=pltpu.CompilerParams(vmem_limit_bytes=48 * MIB),
        cost_estimate=pl.CostEstimate(
            flops=6 * rows * BAND * width, bytes_accessed=rows * width * 12, transcendentals=0
        ),
    )(up, own, down, high, low)


def shift(x, axis, step):
    count = lax.axis_size(axis)
    return lax.ppermute(x, axis, [(i, i + step) for i in range(count) if 0 <= i + step < count])


def row_halo(half):
    return shift(half[-HALO:], "row", 1), shift(half[:HALO], "row", -1)


def body(covariance, *fields):
    levels, block_rows, block_cols = covariance.shape

    def one_level(field, *level):
        lat, lon, up, cour, flon, flat = level
        west = shift(field[:, block_cols - HALO :], "col", 1)
        east = shift(field[:, :HALO], "col", -1)
        source, weight = operator_taps(lat[0], lon[0], up[0], cour[0], flon, flat)
        col0 = lax.axis_index("col") * block_cols
        row0 = lax.axis_index("row") * block_rows
        cut = lambda a, at, size: lax.dynamic_slice(a, (0, at), (TAPS, size))
        col_high, col_low = build_bands(cut(source, col0, block_cols), cut(weight, col0, block_cols), False)
        row_high, row_low = build_bands(cut(source, row0, block_rows), cut(weight, row0, block_rows), True)
        pairs = block_cols // PAIR
        edge_pairs = EDGE // PAIR
        inner_pairs = pairs - 2 * edge_pairs
        reach = BAND - PAIR
        done = []
        if inner_pairs:
            inner = apply_right([(field, 0, block_cols)], col_high, col_low, edge_pairs, inner_pairs)
            up_in, down_in = row_halo(inner)
            done.append(apply_left(up_in, inner, down_in, row_high, row_low))
        left = apply_right([(west, 0, HALO), (field, 0, reach)], col_high, col_low, 0, edge_pairs)
        right = apply_right(
            [(field, block_cols - reach, reach), (east, 0, HALO)], col_high, col_low, pairs - edge_pairs, edge_pairs
        )
        up_l, down_l = row_halo(left)
        up_r, down_r = row_halo(right)
        out_l = apply_left(up_l, left, down_l, row_high, row_low)
        out_r = apply_left(up_r, right, down_r, row_high, row_low)
        return jnp.concatenate([out_l] + done + [out_r], axis=1)

    return jnp.stack([one_level(covariance[k], *[f[k] for f in fields]) for k in range(levels)])


def solution(mesh):
    in_specs = (P(None, "row", "col"), P(), P(), P(), P(), P(), P())
    out_specs = P(None, "row", "col")
    return jax.shard_map(body, mesh=mesh, in_specs=in_specs, out_specs=out_specs, check_vma=False)
```

time: 1030 us -> 147 us (0.14)
  local copies, waits for them, and re-layouts: 563 us -> 24.6 us
  waiting for transfers between devices: 277 us -> 19.7 us
  blocking collectives: 99.1 us -> 0 us
  Pallas kernels: 0 us -> 70.5 us
  other arithmetic: 71.4 us -> 6.03 us
  starting transfers between devices: 11.9 us -> 24.8 us
    gather x3 -> x0, local copies, waits for them, and re-layouts: 509 us -> none  [predicted_covariance(): picked = jnp.take(field_stack, both_index, axis=1)]
    all_to_all x2 -> x0, waiting for transfers between devices: 277 us -> none  [the longest x1 188 us: body(): lax.all_to_all(outgoing, ('row', 'col'), split_axis=1, concat_axis=3, til...]
    all_to_all x1 -> x0, blocking collectives: 99.1 us -> none  [body(): lax.all_to_all(back_rows, 'col', split_axis=2, concat_axis=1, tiled=True)]
    pallas_call x0 -> x8, Pallas kernels: none -> 70.5 us  [the longest x3 28.2 us: apply_left(): pl.pallas_call(functools.partial(left_kernel, pairs=pairs), grid=(width /...]
    add x9 -> x2, other arithmetic: 45.1 us -> 0.22 us  [operator_taps(): near = (lat_near * NLON + lon_near).reshape(NLAT, NLON)]
    ppermute x0 -> x8, starting transfers between devices: none -> 24.8 us  [shift(): lax.ppermute(x, axis, [(i, i + step) for i in range(count) if 0 <= i + st...]
    ppermute x0 -> x8, waiting for transfers between devices: none -> 19.7 us  [shift(): lax.ppermute(x, axis, [(i, i + step) for i in range(count) if 0 <= i + st...]
    select_n x2 -> x0, other arithmetic: 19.7 us -> none  [predicted_covariance(): picked = jnp.take(field_stack, both_index, axis=1)]
  transfers between devices with their start and end apart: 2 -> 8, of which waited for: 2 -> 1; matrix products, arithmetic and copies ran while one was open for 0% -> 9% of each run, Pallas kernels for 0% -> 43%
where the time goes in v1:
time: 147 us; the launch traced here: 146 us
  Pallas kernels  70.5 us (48%)
  starting transfers between devices  24.8 us (17%)
  local copies, waits for them, and re-layouts  24.6 us (17%)
  waiting for transfers between devices  19.7 us (13%)
  other arithmetic  6.03 us (4%)
    pallas_call x3, Pallas kernels, apply_left(): pl.pallas_call(functools.partial(left_kernel, pairs=pairs), grid=(width /...  28.2 us
    ppermute x8, starting transfers between devices, shift(): lax.ppermute(x, axis, [(i, i + step) for i in range(count) if 0 <= i + st...  24.8 us
    pallas_call x3, Pallas kernels, apply_right(): pl.pallas_call(functools.partial(right_kernel, parts=len(parts), pairs=pa...  24.2 us
    ppermute x8, waiting for transfers between devices, shift(): lax.ppermute(x, axis, [(i, i + step) for i in range(count) if 0 <= i + st...  19.7 us
    pallas_call x2, Pallas kernels, build_bands(): pl.pallas_call(functools.partial(band_kernel, turned=turned), grid=(pairs...  18.1 us
    unnamed x30, local copies, waits for them, and re-layouts  9.12 us
    slice x3, local copies, waits for them, and re-layouts, row_halo(): return (shift(half[-HALO:], 'row', 1), shift(half[:HALO], 'row', -1))  5.12 us
    slice x1, local copies, waits for them, and re-layouts, one_level(): west = shift(field[:, block_cols - HALO:], 'col', 1)  4.68 us
  transfers between devices with their start and end apart: 8, of which 1 were waited for; matrix products, arithmetic and copies ran while one was open for 9% of the time, Pallas kernels for 43%

profile of v1, /device:TPU:1, one launch (start us, length us, event | category | flops | bytes accessed | tf_op | source)
XLA Modules:
  0.0 146.4 jit_solution(10687905177905353969)
XLA Ops:
  0.0 4.7 %fusion.39 = (f32[1024,512]{1,0:T(8,128)}, f32[1024,512]{1,0:T(8,128)}) fusion(f32[1024,2048]{1,0:T(8,128)} %bitcast.106), kind=kLoop, calls=%fused_computation.130 | loop fusion | bytes 8388608 | tf_op jit(solution)/shard_map/slice | solution.py:186
  4.7 5.3 %collective-permute-start = (f32[1024,512]{1,0:T(8,128)}, f32[1024,512]{1,0:T(8,128)}, u32[]{:S(2)}, u32[]{:S(2)}) collective-permute-start(f32[1024,512]{1,0:T(8,128)} %get-tuple-element.17), channel_id=1, source_target_pairs={{0,1},{1,2},{2,3},{4,5},{5,6},{6,7},{8,9},{9,10},{10,11},{12,13},{... | collective-permute-start | bytes 6291464 | tf_op jit(solution)/shard_map/ppermute | solution.py:174
  17.2 11.8 %shard_map.73 = (bf16[8,1280,256]{2,1,0:T(8,128)(2,1)S(1)}, bf16[8,1280,256]{2,1,0:T(8,128)(2,1)S(1)}) custom-call(s32[10,2048]{1,0:T(8,128)S(1)} %constant_dynamic-slice_fusion.3.source_ref, f32[10,2048]{1,0:T(8,128)S(1)} %constant_dynamic-slice_fusion.2.weight_ref), custom_call_target="tpu_custom_call" | custom-call | flops 1258291200 | bytes 10485760 | tf_op jit(solution)/shard_map/pallas_call | solution.py:80
  29.1 2.3 %copy-done.4 = bf16[8,1280,256]{2,1,0:T(8,128)(2,1)} copy-done((bf16[8,1280,256]{2,1,0:T(8,128)(2,1)}, bf16[8,1280,256]{2,1,0:T(8,128)(2,1)S(1)}, u32[]{:S(2)}) %copy-start.4) | copy-done | bytes 5242904
  31.6 1.5 %copy-done.2 = bf16[8,1280,256]{2,1,0:T(8,128)(2,1)} copy-done((bf16[8,1280,256]{2,1,0:T(8,128)(2,1)}, bf16[8,1280,256]{2,1,0:T(8,128)(2,1)S(1)}, u32[]{:S(2)}) %copy-start.2) | copy-done | bytes 5242904
  33.3 11.4 %shard_map.77.own_ref = f32[1024,1024]{1,0:T(8,128)} custom-call(f32[1024,2048]{1,0:T(8,128)} %bitcast.107, bf16[4,1280,256]{2,1,0:T(8,128)(2,1)S(1)} %slice.175.refs_1_, bf16[4,1280,256]{2,1,0:T(8,128)(2,1)S(1)} %slice.176.refs_2_), custom_call_target="tpu_custom_call" | custom-call | flops 8053063680 | bytes 12582912 | tf_op jit(solution)/shard_map/pallas_call | solution.py:122
  44.7 4.8 %fusion.42 = (f32[512,1024]{1,0:T(8,128)}, f32[512,1024]{1,0:T(8,128)}) fusion(f32[1024,1024]{1,0:T(8,128)} %shard_map.77.own_ref), kind=kLoop, calls=%fused_computation.133 | loop fusion | bytes 8388608 | tf_op jit(solution)/shard_map/slice | solution.py:178
  49.5 2.9 %collective-permute-start.4 = (f32[512,1024]{1,0:T(8,128)}, f32[512,1024]{1,0:T(8,128)S(1)}, u32[]{:S(2)}, u32[]{:S(2)}) collective-permute-start(f32[512,1024]{1,0:T(8,128)} %get-tuple-element.23), channel_id=1, source_target_pairs={{4,0},{8,4},{12,8},{16,12},{20,16},{24,20},{28,24},{5,1},{9,5},{13... | collective-permute-start | bytes 6291464 | tf_op jit(solution)/shard_map/ppermute | solution.py:174
  52.3 3.3 %collective-permute-start.3 = (f32[512,1024]{1,0:T(8,128)}, f32[512,1024]{1,0:T(8,128)}, u32[]{:S(2)}, u32[]{:S(2)}) collective-permute-start(f32[512,1024]{1,0:T(8,128)} %get-tuple-element.24), channel_id=1, source_target_pairs={{0,4},{4,8},{8,12},{12,16},{16,20},{20,24},{24,28},{1,5},{5,9},{9,... | collective-permute-start | bytes 6291464 | tf_op jit(solution)/shard_map/ppermute | solution.py:174
  55.7 2.0 %fusion.41 = (bf16[2,1280,256]{2,1,0:T(8,128)(2,1)S(1)}, bf16[2,1280,256]{2,1,0:T(8,128)(2,1)S(1)}) fusion(bf16[8,1280,256]{2,1,0:T(8,128)(2,1)} %copy-done.4), kind=kLoop, calls=%fused_computation.132 | loop fusion | bytes 5242880 | tf_op jit(solution)/shard_map/slice | solution.py:119
  57.7 6.3 %shard_map.75 = (bf16[4,256,1280]{2,1,0:T(8,128)(2,1)S(1)}, bf16[4,256,1280]{2,1,0:T(8,128)(2,1)S(1)}) custom-call(s32[10,1024]{1,0:T(8,128)S(1)} %constant_dynamic-slice_fusion.1.source_ref, f32[10,1024]{1,0:T(8,128)S(1)} %constant_dynamic-slice_fusion.weight_ref), custom_call_target="tpu_custom_call" | custom-call | flops 629145600 | bytes 5242880 | tf_op jit(solution)/shard_map/pallas_call | solution.py:80
  64.1 1.5 %copy-done.6 = bf16[4,256,1280]{2,1,0:T(8,128)(2,1)} copy-done((bf16[4,256,1280]{2,1,0:T(8,128)(2,1)}, bf16[4,256,1280]{2,1,0:T(8,128)(2,1)S(1)}, u32[]{:S(2)}) %copy-start.6) | copy-done | bytes 2621464
  65.8 1.3 copy-done.5
  67.1 6.4 %shard_map.74.own_ref = f32[1024,512]{1,0:T(8,128)S(1)} custom-call(f32[1024,512]{1,0:T(8,128)} %collective-permute-done.refs_0_, f32[1024,2048]{1,0:T(8,128)} %bitcast.108, bf16[2,1280,256]{2,1,0:T(8,128)(2,1)S(1)} %get-tuple-element.21.refs_2_, bf16[2,1280,256]{2,1,0:T(8,128)(2,1)S(1)} %get-tuple-element.19.refs_3_), custom_call_target="tpu_custom_call" | custom-call | flops 4026531840 | bytes 6291456 | tf_op jit(solution)/shard_map/pallas_call | solution.py:122
  74.8 2.4 %collective-permute-start.2 = (f32[512,512]{1,0:T(8,128)S(1)}, f32[512,512]{1,0:T(8,128)S(1)}, u32[]{:S(2)}, u32[]{:S(2)}) collective-permute-start(f32[512,512]{1,0:T(8,128)S(1)} %get-tuple-element.25), channel_id=1, source_target_pairs={{4,0},{8,4},{12,8},{16,12},{20,16},{24,20},{28,24},{5,1},{9,5},{13... | collective-permute-start | bytes 3145736 | tf_op jit(solution)/shard_map/ppermute | solution.py:174
  77.2 3.2 %collective-permute-start.1 = (f32[512,512]{1,0:T(8,128)S(1)}, f32[512,512]{1,0:T(8,128)S(1)}, u32[]{:S(2)}, u32[]{:S(2)}) collective-permute-start(f32[512,512]{1,0:T(8,128)S(1)} %get-tuple-element.26), channel_id=1, source_target_pairs={{0,4},{4,8},{8,12},{12,16},{16,20},{20,24},{24,28},{1,5},{5,9},{9,... | collective-permute-start | bytes 3145736 | tf_op jit(solution)/shard_map/ppermute | solution.py:174
  80.4 19.7 %collective-permute-done.5.refs_1_ = f32[1024,512]{1,0:T(8,128)} collective-permute-done((f32[1024,512]{1,0:T(8,128)}, f32[1024,512]{1,0:T(8,128)}, u32[]{:S(2)}, u32[]{:S(2)}) %collective-permute-start.5) | collective-permute-done | bytes 2097184 | tf_op jit(solution)/shard_map/ppermute | solution.py:174
  100.1 6.3 %shard_map.79.own_ref = f32[1024,512]{1,0:T(8,128)S(1)} custom-call(f32[1024,2048]{1,0:T(8,128)} %bitcast.109, f32[1024,512]{1,0:T(8,128)} %collective-permute-done.5.refs_1_, bf16[2,1280,256]{2,1,0:T(8,128)(2,1)S(1)} %get-tuple-element.22.refs_2_, bf16[2,1280,256]{2,1,0:T(8,128)(2,1)S(1)} %get-tuple-element.20.refs_3_), custom_call_target="tpu_custom_call" | custom-call | flops 4026531840 | bytes 6291456 | tf_op jit(solution)/shard_map/pallas_call | solution.py:122
  107.8 3.4 %collective-permute-start.7 = (f32[512,512]{1,0:T(8,128)S(1)}, f32[512,512]{1,0:T(8,128)S(1)}, u32[]{:S(2)}, u32[]{:S(2)}) collective-permute-start(f32[512,512]{1,0:T(8,128)S(1)} %get-tuple-element.27), channel_id=1, source_target_pairs={{4,0},{8,4},{12,8},{16,12},{20,16},{24,20},{28,24},{5,1},{9,5},{13... | collective-permute-start | bytes 3145736 | tf_op jit(solution)/shard_map/ppermute | solution.py:174
  111.2 3.1 %collective-permute-start.6 = (f32[512,512]{1,0:T(8,128)S(1)}, f32[512,512]{1,0:T(8,128)S(1)}, u32[]{:S(2)}, u32[]{:S(2)}) collective-permute-start(f32[512,512]{1,0:T(8,128)S(1)} %get-tuple-element.28), channel_id=1, source_target_pairs={{0,4},{4,8},{8,12},{12,16},{16,20},{20,24},{24,28},{1,5},{5,9},{9,... | collective-permute-start | bytes 3145736 | tf_op jit(solution)/shard_map/ppermute | solution.py:174
  114.4 13.1 %shard_map.78 = f32[1024,1024]{1,0:T(8,128)} custom-call(f32[512,1024]{1,0:T(8,128)} %collective-permute-done.3.up_ref, f32[1024,1024]{1,0:T(8,128)} %shard_map.77.own_ref, f32[512,1024]{1,0:T(8,128)S(1)} %collective-permute-done.4.down_ref, bf16[4,256,1280]{2,1,0:T(8,128)(2,1)} %copy-done.5, bf16[4,256,1280]{2,1,0:T(8,128)(2,1)} %copy-done.6), custom_call_target="tpu_custom_call" | custom-call | flops 8053063680 | bytes 12582912 | tf_op jit(solution)/shard_map/pallas_call | solution.py:153
  127.4 7.5 %shard_map.76 = f32[1024,512]{1,0:T(8,128)S(1)} custom-call(f32[512,512]{1,0:T(8,128)S(1)} %collective-permute-done.1.up_ref, f32[1024,512]{1,0:T(8,128)} %copy-done, f32[512,512]{1,0:T(8,128)S(1)} %collective-permute-done.2.down_ref, bf16[4,256,1280]{2,1,0:T(8,128)(2,1)} %copy-done.5, bf16[4,256,1280]{2,1,0:T(8,128)(2,1)} %copy-done.6), custom_call_target="tpu_custom_call" | custom-call | flops 4026531840 | bytes 6291456 | tf_op jit(solution)/shard_map/pallas_call | solution.py:153
  135.0 7.6 %shard_map.80 = f32[1024,512]{1,0:T(8,128)S(1)} custom-call(f32[512,512]{1,0:T(8,128)S(1)} %collective-permute-done.6.up_ref, f32[1024,512]{1,0:T(8,128)} %copy-done.1, f32[512,512]{1,0:T(8,128)S(1)} %collective-permute-done.7.down_ref, bf16[4,256,1280]{2,1,0:T(8,128)(2,1)} %copy-done.5, bf16[4,256,1280]{2,1,0:T(8,128)(2,1)} %copy-done.6), custom_call_target="tpu_custom_call" | custom-call | flops 4026531840 | bytes 6291456 | tf_op jit(solution)/shard_map/pallas_call | solution.py:153
  142.6 3.7 %maximum_bitcast_fusion = f32[1,1024,2048]{2,1,0:T(8,128)} fusion(f32[1024,512]{1,0:T(8,128)S(1)} %shard_map.80, f32[1024,1024]{1,0:T(8,128)S(1)} %copy-done.7, f32[1024,512]{1,0:T(8,128)S(1)} %shard_map.76), kind=kLoop, calls=%fused_computation | loop fusion | flops 4194304 | bytes 16777216 | tf_op jit(solution)/shard_map/stack | solution.py:213
  (100 shorter events, 10.0 us)
Async XLA Ops:
  0.0 11.3 %copy-start.8 = (f32[1,1,8192]{2,1,0:T(1,128)S(1)}, f32[1,1,8192]{2,1,0:T(1,128)}, u32[]{:S(2)}) copy-start(f32[1,1,8192]{2,1,0:T(1,128)} %param.11) | copy-start | bytes 98308
  0.0 11.6 %copy-start.9 = (s32[1,1,8192]{2,1,0:T(1,128)S(1)}, s32[1,1,8192]{2,1,0:T(1,128)}, u32[]{:S(2)}) copy-start(s32[1,1,8192]{2,1,0:T(1,128)} %param.8) | copy-start | bytes 98308
  0.0 11.7 %copy-start.11 = (s32[1,1,8192]{2,1,0:T(1,128)S(1)}, s32[1,1,8192]{2,1,0:T(1,128)}, u32[]{:S(2)}) copy-start(s32[1,1,8192]{2,1,0:T(1,128)} %param.10) | copy-start | bytes 98308
  0.0 11.8 %copy-start.10 = (s32[1,1,8192]{2,1,0:T(1,128)S(1)}, s32[1,1,8192]{2,1,0:T(1,128)}, u32[]{:S(2)}) copy-start(s32[1,1,8192]{2,1,0:T(1,128)} %param.9) | copy-start | bytes 98308
  4.7 62.4 %collective-permute-start = (f32[1024,512]{1,0:T(8,128)}, f32[1024,512]{1,0:T(8,128)}, u32[]{:S(2)}, u32[]{:S(2)}) collective-permute-start(f32[1024,512]{1,0:T(8,128)} %get-tuple-element.17), channel_id=1, source_target_pairs={{0,1},{1,2},{2,3},{4,5},{5,6},{6,7},{8,9},{9,10},{10,11},{12,13},{... | collective-permute-start | bytes 6291464 | tf_op jit(solution)/shard_map/ppermute | solution.py:174
  10.0 90.1 %collective-permute-start.5 = (f32[1024,512]{1,0:T(8,128)}, f32[1024,512]{1,0:T(8,128)}, u32[]{:S(2)}, u32[]{:S(2)}) collective-permute-start(f32[1024,512]{1,0:T(8,128)} %get-tuple-element.18), channel_id=1, source_target_pairs={{1,0},{2,1},{3,2},{5,4},{6,5},{7,6},{9,8},{10,9},{11,10},{13,12},{... | collective-permute-start | bytes 6291464 | tf_op jit(solution)/shard_map/ppermute | solution.py:174
  13.1 2.8 %copy-start.12 = (f32[1,8192]{1,0:T(1,128)S(1)}, f32[1,8192]{1,0:T(1,128)}, u32[]{:S(2)}) copy-start(f32[1,8192]{1,0:T(1,128)} %param.13) | copy-start | bytes 98308
  13.1 2.9 %copy-start.13 = (f32[1,8192]{1,0:T(1,128)S(1)}, f32[1,8192]{1,0:T(1,128)}, u32[]{:S(2)}) copy-start(f32[1,8192]{1,0:T(1,128)} %param.12) | copy-start | bytes 98308
  29.0 2.4 %copy-start.4 = (bf16[8,1280,256]{2,1,0:T(8,128)(2,1)}, bf16[8,1280,256]{2,1,0:T(8,128)(2,1)S(1)}, u32[]{:S(2)}) copy-start(bf16[8,1280,256]{2,1,0:T(8,128)(2,1)S(1)} %get-tuple-element.9) | copy-start | bytes 15728644
  29.1 4.0 %copy-start.2 = (bf16[8,1280,256]{2,1,0:T(8,128)(2,1)}, bf16[8,1280,256]{2,1,0:T(8,128)(2,1)S(1)}, u32[]{:S(2)}) copy-start(bf16[8,1280,256]{2,1,0:T(8,128)(2,1)S(1)} %get-tuple-element.10) | copy-start | bytes 15728644
  49.5 61.8 %collective-permute-start.4 = (f32[512,1024]{1,0:T(8,128)}, f32[512,1024]{1,0:T(8,128)S(1)}, u32[]{:S(2)}, u32[]{:S(2)}) collective-permute-start(f32[512,1024]{1,0:T(8,128)} %get-tuple-element.23), channel_id=1, source_target_pairs={{4,0},{8,4},{12,8},{16,12},{20,16},{24,20},{28,24},{5,1},{9,5},{13... | collective-permute-start | bytes 6291464 | tf_op jit(solution)/shard_map/ppermute | solution.py:174
  52.3 62.0 %collective-permute-start.3 = (f32[512,1024]{1,0:T(8,128)}, f32[512,1024]{1,0:T(8,128)}, u32[]{:S(2)}, u32[]{:S(2)}) collective-permute-start(f32[512,1024]{1,0:T(8,128)} %get-tuple-element.24), channel_id=1, source_target_pairs={{0,4},{4,8},{8,12},{12,16},{16,20},{20,24},{24,28},{1,5},{5,9},{9,... | collective-permute-start | bytes 6291464 | tf_op jit(solution)/shard_map/ppermute | solution.py:174
  55.7 9.9 %copy-start.3 = (bf16[8,1280,256]{2,1,0:T(8,128)(2,1)S(1)}, bf16[8,1280,256]{2,1,0:T(8,128)(2,1)}, u32[]{:S(2)}) copy-start(bf16[8,1280,256]{2,1,0:T(8,128)(2,1)} %copy-done.2) | copy-start | bytes 15728644
  64.1 1.5 %copy-start.6 = (bf16[4,256,1280]{2,1,0:T(8,128)(2,1)}, bf16[4,256,1280]{2,1,0:T(8,128)(2,1)S(1)}, u32[]{:S(2)}) copy-start(bf16[4,256,1280]{2,1,0:T(8,128)(2,1)S(1)} %get-tuple-element.12.low_ref) | copy-start | bytes 7864324
  65.6 1.5 %copy-start.5 = (bf16[4,256,1280]{2,1,0:T(8,128)(2,1)}, bf16[4,256,1280]{2,1,0:T(8,128)(2,1)S(1)}, u32[]{:S(2)}) copy-start(bf16[4,256,1280]{2,1,0:T(8,128)(2,1)S(1)} %get-tuple-element.11.high_ref) | copy-start | bytes 7864324
  73.5 1.3 copy-start
  74.8 52.6 %collective-permute-start.2 = (f32[512,512]{1,0:T(8,128)S(1)}, f32[512,512]{1,0:T(8,128)S(1)}, u32[]{:S(2)}, u32[]{:S(2)}) collective-permute-start(f32[512,512]{1,0:T(8,128)S(1)} %get-tuple-element.25), channel_id=1, source_target_pairs={{4,0},{8,4},{12,8},{16,12},{20,16},{24,20},{28,24},{5,1},{9,5},{13... | collective-permute-start | bytes 3145736 | tf_op jit(solution)/shard_map/ppermute | solution.py:174
  77.2 50.2 %collective-permute-start.1 = (f32[512,512]{1,0:T(8,128)S(1)}, f32[512,512]{1,0:T(8,128)S(1)}, u32[]{:S(2)}, u32[]{:S(2)}) collective-permute-start(f32[512,512]{1,0:T(8,128)S(1)} %get-tuple-element.26), channel_id=1, source_target_pairs={{0,4},{4,8},{8,12},{12,16},{16,20},{20,24},{24,28},{1,5},{5,9},{9,... | collective-permute-start | bytes 3145736 | tf_op jit(solution)/shard_map/ppermute | solution.py:174
  106.5 1.3 copy-start.1
  107.8 27.2 %collective-permute-start.7 = (f32[512,512]{1,0:T(8,128)S(1)}, f32[512,512]{1,0:T(8,128)S(1)}, u32[]{:S(2)}, u32[]{:S(2)}) collective-permute-start(f32[512,512]{1,0:T(8,128)S(1)} %get-tuple-element.27), channel_id=1, source_target_pairs={{4,0},{8,4},{12,8},{16,12},{20,16},{24,20},{28,24},{5,1},{9,5},{13... | collective-permute-start | bytes 3145736 | tf_op jit(solution)/shard_map/ppermute | solution.py:174
  111.2 23.7 %collective-permute-start.6 = (f32[512,512]{1,0:T(8,128)S(1)}, f32[512,512]{1,0:T(8,128)S(1)}, u32[]{:S(2)}, u32[]{:S(2)}) collective-permute-start(f32[512,512]{1,0:T(8,128)S(1)} %get-tuple-element.28), channel_id=1, source_target_pairs={{0,4},{4,8},{8,12},{12,16},{16,20},{20,24},{24,28},{1,5},{5,9},{9,... | collective-permute-start | bytes 3145736 | tf_op jit(solution)/shard_map/ppermute | solution.py:174
  135.0 7.7 %copy-start.7 = (f32[1024,1024]{1,0:T(8,128)S(1)}, f32[1024,1024]{1,0:T(8,128)}, u32[]{:S(2)}) copy-start(f32[1024,1024]{1,0:T(8,128)} %shard_map.78) | copy-start | bytes 12582916

commit v2 on v1

--- a/solution.py
+++ b/solution.py
@@ -132,7 +132,8 @@
     )(*[p[0] for p in parts], high, low)
 
 
-def left_kernel(up_ref, own_ref, down_ref, high_ref, low_ref, out_ref, *, pairs):
+def left_kernel(up_ref, own_ref, down_ref, high_ref, low_ref, *rest, pairs):
+    out_ref = rest[-1]
     split = [halves(r[...]) for r in (up_ref, own_ref, down_ref)]
     high = jnp.concatenate([s[0] for s in split], axis=0)
     low = jnp.concatenate([s[1] for s in split], axis=0)
@@ -144,7 +145,8 @@
         )
 
 
-def apply_left(up, own, down, high, low, tile=256):
+def apply_left(up, own, down, high, low, start, total, before, tile=256):
+    kept = [] if before is None else [before]
     rows, width = own.shape
     tile = min(tile, width)
     pairs = rows // PAIR
@@ -159,14 +161,16 @@
             pl.BlockSpec((HALO, tile), column),
             bands,
             bands,
-        ],
-        out_specs=pl.BlockSpec((rows, tile), column),
-        out_shape=jax.ShapeDtypeStruct((rows, width), jnp.float32),
+        ]
+        + [pl.BlockSpec(memory_space=pl.ANY)] * len(kept),
+        out_specs=pl.BlockSpec((rows, tile), lambda i: (0, start // tile + i)),
+        out_shape=jax.ShapeDtypeStruct((rows, total), jnp.float32),
+        input_output_aliases={5: 0} if kept else {},
         compiler_params=pltpu.CompilerParams(vmem_limit_bytes=48 * MIB),
         cost_estimate=pl.CostEstimate(
             flops=6 * rows * BAND * width, bytes_accessed=rows * width * 12, transcendentals=0
         ),
-    )(up, own, down, high, low)
+    )(up, own, down, high, low, *kept)
 
 
 def shift(x, axis, step):
@@ -195,20 +199,19 @@
         edge_pairs = EDGE // PAIR
         inner_pairs = pairs - 2 * edge_pairs
         reach = BAND - PAIR
-        done = []
+        result = None
         if inner_pairs:
             inner = apply_right([(field, 0, block_cols)], col_high, col_low, edge_pairs, inner_pairs)
             up_in, down_in = row_halo(inner)
-            done.append(apply_left(up_in, inner, down_in, row_high, row_low))
+            result = apply_left(up_in, inner, down_in, row_high, row_low, EDGE, block_cols, None)
         left = apply_right([(west, 0, HALO), (field, 0, reach)], col_high, col_low, 0, edge_pairs)
         right = apply_right(
             [(field, block_cols - reach, reach), (east, 0, HALO)], col_high, col_low, pairs - edge_pairs, edge_pairs
         )
         up_l, down_l = row_halo(left)
         up_r, down_r = row_halo(right)
-        out_l = apply_left(up_l, left, down_l, row_high, row_low)
-        out_r = apply_left(up_r, right, down_r, row_high, row_low)
-        return jnp.concatenate([out_l] + done + [out_r], axis=1)
+        result = apply_left(up_l, left, down_l, row_high, row_low, 0, block_cols, result)
+        return apply_left(up_r, right, down_r, row_high, row_low, block_cols - EDGE, block_cols, result)
 
     return jnp.stack([one_level(covariance[k], *[f[k] for f in fields]) for k in range(levels)])
 

time: 147 us -> 144 us (0.980)
  other arithmetic: 6.03 us -> 2.29 us
  local copies, waits for them, and re-layouts: 24.6 us -> 22.7 us
  waiting for transfers between devices: 19.7 us -> 21.5 us
    another operation x1 -> x0, other arithmetic: 3.74 us -> none  [body(): jnp.stack([one_level(covariance[k], *[f[k] for f in fields]) for k in ran...]
    unnamed x30 -> x24, local copies, waits for them, and re-layouts: 9.12 us -> 6.19 us
    ppermute x8, waiting for transfers between devices: 19.7 us -> 21.5 us  [shift(): lax.ppermute(x, axis, [(i, i + step) for i in range(count) if 0 <= i + st...]
  transfers between devices with their start and end apart: 8 -> 8, of which waited for: 1 -> 1; matrix products, arithmetic and copies ran while one was open for 9% -> 10% of each run, Pallas kernels for 43% -> 44%
where the time goes in v2:
time: 144 us
  Pallas kernels  71.7 us (50%)
  starting transfers between devices  24.8 us (17%)
  local copies, waits for them, and re-layouts  22.7 us (16%)
  waiting for transfers between devices  21.5 us (15%)
  other arithmetic  2.29 us (2%)
    pallas_call x3, Pallas kernels, apply_left(): pl.pallas_call(functools.partial(left_kernel, pairs=pairs), grid=(width /...  29.3 us
    ppermute x8, starting transfers between devices, shift(): lax.ppermute(x, axis, [(i, i + step) for i in range(count) if 0 <= i + st...  24.8 us
    pallas_call x3, Pallas kernels, apply_right(): pl.pallas_call(functools.partial(right_kernel, parts=len(parts), pairs=pa...  24.2 us
    ppermute x8, waiting for transfers between devices, shift(): lax.ppermute(x, axis, [(i, i + step) for i in range(count) if 0 <= i + st...  21.5 us
    pallas_call x2, Pallas kernels, build_bands(): pl.pallas_call(functools.partial(band_kernel, turned=turned), grid=(pairs...  18.1 us
    unnamed x24, local copies, waits for them, and re-layouts  6.19 us
    slice x3, local copies, waits for them, and re-layouts, row_halo(): return (shift(half[-HALO:], 'row', 1), shift(half[:HALO], 'row', -1))  6.09 us
    slice x1, local copies, waits for them, and re-layouts, one_level(): west = shift(field[:, block_cols - HALO:], 'col', 1)  4.75 us
  transfers between devices with their start and end apart: 8, of which 1 were waited for; matrix products, arithmetic and copies ran while one was open for 10% of the time, Pallas kernels for 44%

profile of v2, /device:TPU:1, one launch (start us, length us, event | category | flops | bytes accessed | tf_op | source)
XLA Modules:
  0.0 143.6 jit_solution(15708396188417545402)
XLA Ops:
  0.0 4.7 %fusion.39 = (f32[1024,512]{1,0:T(8,128)}, f32[1024,512]{1,0:T(8,128)}) fusion(f32[1024,2048]{1,0:T(8,128)} %bitcast.105), kind=kLoop, calls=%fused_computation.129 | loop fusion | bytes 8388608 | tf_op jit(solution)/shard_map/slice | solution.py:190
  4.8 5.3 %collective-permute-start.3 = (f32[1024,512]{1,0:T(8,128)}, f32[1024,512]{1,0:T(8,128)}, u32[]{:S(2)}, u32[]{:S(2)}) collective-permute-start(f32[1024,512]{1,0:T(8,128)} %get-tuple-element.17), channel_id=1, source_target_pairs={{0,1},{1,2},{2,3},{4,5},{5,6},{6,7},{8,9},{9,10},{10,11},{12,13},{... | collective-permute-start | bytes 6291464 | tf_op jit(solution)/shard_map/ppermute | solution.py:178
  10.0 1.3 collective-permute-start
  17.3 11.8 %shard_map.73 = (bf16[8,1280,256]{2,1,0:T(8,128)(2,1)S(1)}, bf16[8,1280,256]{2,1,0:T(8,128)(2,1)S(1)}) custom-call(s32[10,2048]{1,0:T(8,128)S(1)} %constant_dynamic-slice_fusion.3.source_ref, f32[10,2048]{1,0:T(8,128)S(1)} %constant_dynamic-slice_fusion.2.weight_ref), custom_call_target="tpu_custom_call" | custom-call | flops 1258291200 | bytes 10485760 | tf_op jit(solution)/shard_map/pallas_call | solution.py:80
  29.1 2.3 %copy-done.4 = bf16[8,1280,256]{2,1,0:T(8,128)(2,1)} copy-done((bf16[8,1280,256]{2,1,0:T(8,128)(2,1)}, bf16[8,1280,256]{2,1,0:T(8,128)(2,1)S(1)}, u32[]{:S(2)}) %copy-start.4) | copy-done | bytes 5242904
  31.6 1.5 %copy-done.2 = bf16[8,1280,256]{2,1,0:T(8,128)(2,1)} copy-done((bf16[8,1280,256]{2,1,0:T(8,128)(2,1)}, bf16[8,1280,256]{2,1,0:T(8,128)(2,1)S(1)}, u32[]{:S(2)}) %copy-start.2) | copy-done | bytes 5242904
  33.3 11.5 %shard_map.77.own_ref = f32[1024,1024]{1,0:T(8,128)} custom-call(f32[1024,2048]{1,0:T(8,128)} %bitcast.106, bf16[4,1280,256]{2,1,0:T(8,128)(2,1)S(1)} %slice.180.refs_1_, bf16[4,1280,256]{2,1,0:T(8,128)(2,1)S(1)} %slice.181.refs_2_), custom_call_target="tpu_custom_call" | custom-call | flops 8053063680 | bytes 12582912 | tf_op jit(solution)/shard_map/pallas_call | solution.py:122
  44.8 4.8 %fusion.42 = (f32[512,1024]{1,0:T(8,128)}, f32[512,1024]{1,0:T(8,128)}) fusion(f32[1024,1024]{1,0:T(8,128)} %shard_map.77.own_ref), kind=kLoop, calls=%fused_computation.132 | loop fusion | bytes 8388608 | tf_op jit(solution)/shard_map/slice | solution.py:182
  49.6 2.8 %collective-permute-start.7 = (f32[512,1024]{1,0:T(8,128)}, f32[512,1024]{1,0:T(8,128)S(1)}, u32[]{:S(2)}, u32[]{:S(2)}) collective-permute-start(f32[512,1024]{1,0:T(8,128)} %get-tuple-element.23), channel_id=1, source_target_pairs={{4,0},{8,4},{12,8},{16,12},{20,16},{24,20},{28,24},{5,1},{9,5},{13... | collective-permute-start | bytes 6291464 | tf_op jit(solution)/shard_map/ppermute | solution.py:178
  52.4 3.3 %collective-permute-start.6 = (f32[512,1024]{1,0:T(8,128)}, f32[512,1024]{1,0:T(8,128)}, u32[]{:S(2)}, u32[]{:S(2)}) collective-permute-start(f32[512,1024]{1,0:T(8,128)} %get-tuple-element.24), channel_id=1, source_target_pairs={{0,4},{4,8},{8,12},{12,16},{16,20},{20,24},{24,28},{1,5},{5,9},{9,... | collective-permute-start | bytes 6291464 | tf_op jit(solution)/shard_map/ppermute | solution.py:178
  55.7 2.0 %fusion.41 = (bf16[2,1280,256]{2,1,0:T(8,128)(2,1)S(1)}, bf16[2,1280,256]{2,1,0:T(8,128)(2,1)S(1)}) fusion(bf16[8,1280,256]{2,1,0:T(8,128)(2,1)} %copy-done.4), kind=kLoop, calls=%fused_computation.131 | loop fusion | bytes 5242880 | tf_op jit(solution)/shard_map/slice | solution.py:119
  57.8 6.3 %shard_map.75 = (bf16[4,256,1280]{2,1,0:T(8,128)(2,1)S(1)}, bf16[4,256,1280]{2,1,0:T(8,128)(2,1)S(1)}) custom-call(s32[10,1024]{1,0:T(8,128)S(1)} %constant_dynamic-slice_fusion.1.source_ref, f32[10,1024]{1,0:T(8,128)S(1)} %constant_dynamic-slice_fusion.weight_ref), custom_call_target="tpu_custom_call" | custom-call | flops 629145600 | bytes 5242880 | tf_op jit(solution)/shard_map/pallas_call | solution.py:80
  64.4 1.3 copy-done
  66.5 6.4 %shard_map.76.own_ref = f32[1024,512]{1,0:T(8,128)S(1)} custom-call(f32[1024,512]{1,0:T(8,128)} %collective-permute-done.3.refs_0_, f32[1024,2048]{1,0:T(8,128)} %bitcast.107, bf16[2,1280,256]{2,1,0:T(8,128)(2,1)S(1)} %get-tuple-element.21.refs_2_, bf16[2,1280,256]{2,1,0:T(8,128)(2,1)S(1)} %get-tuple-element.19.refs_3_), custom_call_target="tpu_custom_call" | custom-call | flops 4026531840 | bytes 6291456 | tf_op jit(solution)/shard_map/pallas_call | solution.py:122
  73.1 2.3 %collective-permute-start.5 = (f32[512,512]{1,0:T(8,128)S(1)}, f32[512,512]{1,0:T(8,128)S(1)}, u32[]{:S(2)}, u32[]{:S(2)}) collective-permute-start(f32[512,512]{1,0:T(8,128)S(1)} %get-tuple-element.25), channel_id=1, source_target_pairs={{4,0},{8,4},{12,8},{16,12},{20,16},{24,20},{28,24},{5,1},{9,5},{13... | collective-permute-start | bytes 3145736 | tf_op jit(solution)/shard_map/ppermute | solution.py:178
  75.4 3.2 %collective-permute-start.4 = (f32[512,512]{1,0:T(8,128)S(1)}, f32[512,512]{1,0:T(8,128)S(1)}, u32[]{:S(2)}, u32[]{:S(2)}) collective-permute-start(f32[512,512]{1,0:T(8,128)S(1)} %get-tuple-element.26), channel_id=1, source_target_pairs={{0,4},{4,8},{8,12},{12,16},{16,20},{20,24},{24,28},{1,5},{5,9},{9,... | collective-permute-start | bytes 3145736 | tf_op jit(solution)/shard_map/ppermute | solution.py:178
  78.7 21.5 %collective-permute-done.refs_1_ = f32[1024,512]{1,0:T(8,128)} collective-permute-done((f32[1024,512]{1,0:T(8,128)}, f32[1024,512]{1,0:T(8,128)}, u32[]{:S(2)}, u32[]{:S(2)}) %collective-permute-start) | collective-permute-done | bytes 2097184 | tf_op jit(solution)/shard_map/ppermute | solution.py:178
  100.2 6.3 %shard_map.74.own_ref = f32[1024,512]{1,0:T(8,128)S(1)} custom-call(f32[1024,2048]{1,0:T(8,128)} %bitcast.108, f32[1024,512]{1,0:T(8,128)} %collective-permute-done.refs_1_, bf16[2,1280,256]{2,1,0:T(8,128)(2,1)S(1)} %get-tuple-element.22.refs_2_, bf16[2,1280,256]{2,1,0:T(8,128)(2,1)S(1)} %get-tuple-element.20.refs_3_), custom_call_target="tpu_custom_call" | custom-call | flops 4026531840 | bytes 6291456 | tf_op jit(solution)/shard_map/pallas_call | solution.py:122
  106.5 1.1 fusion.44
  107.7 3.4 %collective-permute-start.2 = (f32[512,512]{1,0:T(8,128)}, f32[512,512]{1,0:T(8,128)S(1)}, u32[]{:S(2)}, u32[]{:S(2)}) collective-permute-start(f32[512,512]{1,0:T(8,128)} %get-tuple-element.27), channel_id=1, source_target_pairs={{4,0},{8,4},{12,8},{16,12},{20,16},{24,20},{28,24},{5,1},{9,5},{13... | collective-permute-start | bytes 3145736 | tf_op jit(solution)/shard_map/ppermute | solution.py:178
  111.1 3.1 %collective-permute-start.1 = (f32[512,512]{1,0:T(8,128)S(1)}, f32[512,512]{1,0:T(8,128)S(1)}, u32[]{:S(2)}, u32[]{:S(2)}) collective-permute-start(f32[512,512]{1,0:T(8,128)S(1)} %get-tuple-element.28), channel_id=1, source_target_pairs={{0,4},{4,8},{8,12},{12,16},{16,20},{20,24},{24,28},{1,5},{5,9},{9,... | collective-permute-start | bytes 3145736 | tf_op jit(solution)/shard_map/ppermute | solution.py:178
  114.3 13.1 %shard_map.78.rest_0_ = f32[1024,2048]{1,0:T(8,128)} custom-call(f32[512,1024]{1,0:T(8,128)} %collective-permute-done.6.up_ref, f32[1024,1024]{1,0:T(8,128)} %shard_map.77.own_ref, f32[512,1024]{1,0:T(8,128)S(1)} %collective-permute-done.7.down_ref, bf16[4,256,1280]{2,1,0:T(8,128)(2,1)} %copy-done, bf16[4,256,1280]{2,1,0:T(8,128)(2,1)} %copy-done.1), custom_call_target="tpu_custom_call" | custom-call | flops 8053063680 | bytes 12582912 | tf_op jit(solution)/shard_map/pallas_call | solution.py:155
  127.3 8.1 %shard_map.79.rest_0_ = f32[1024,2048]{1,0:T(8,128)} custom-call(f32[512,512]{1,0:T(8,128)S(1)} %collective-permute-done.4.up_ref, f32[1024,512]{1,0:T(8,128)S(1)} %shard_map.76.own_ref, f32[512,512]{1,0:T(8,128)S(1)} %collective-permute-done.5.down_ref, bf16[4,256,1280]{2,1,0:T(8,128)(2,1)} %copy-done, ...), custom_call_target="tpu_custom_call", output_to_operand_aliasing={{}: (5, {})} | custom-call | flops 4026531840 | bytes 6291456 | tf_op jit(solution)/shard_map/pallas_call | solution.py:155
  135.5 8.1 %shard_map.80 = f32[1024,2048]{1,0:T(8,128)} custom-call(f32[512,512]{1,0:T(8,128)S(1)} %collective-permute-done.1.up_ref, f32[1024,512]{1,0:T(8,128)S(1)} %shard_map.74.own_ref, f32[512,512]{1,0:T(8,128)S(1)} %collective-permute-done.2.down_ref, bf16[4,256,1280]{2,1,0:T(8,128)(2,1)} %copy-done, ...), custom_call_target="tpu_custom_call", output_to_operand_aliasing={{}: (5, {})} | custom-call | flops 4026531840 | bytes 6291456 | tf_op jit(solution)/shard_map/pallas_call | solution.py:155
  (93 shorter events, 7.2 us)
Async XLA Ops:
  0.0 11.3 %copy-start.5 = (f32[1,1,8192]{2,1,0:T(1,128)S(1)}, f32[1,1,8192]{2,1,0:T(1,128)}, u32[]{:S(2)}) copy-start(f32[1,1,8192]{2,1,0:T(1,128)} %param.11) | copy-start | bytes 98308
  0.0 11.6 %copy-start.6 = (s32[1,1,8192]{2,1,0:T(1,128)S(1)}, s32[1,1,8192]{2,1,0:T(1,128)}, u32[]{:S(2)}) copy-start(s32[1,1,8192]{2,1,0:T(1,128)} %param.8) | copy-start | bytes 98308
  0.0 11.7 %copy-start.8 = (s32[1,1,8192]{2,1,0:T(1,128)S(1)}, s32[1,1,8192]{2,1,0:T(1,128)}, u32[]{:S(2)}) copy-start(s32[1,1,8192]{2,1,0:T(1,128)} %param.10) | copy-start | bytes 98308
  0.0 11.8 %copy-start.7 = (s32[1,1,8192]{2,1,0:T(1,128)S(1)}, s32[1,1,8192]{2,1,0:T(1,128)}, u32[]{:S(2)}) copy-start(s32[1,1,8192]{2,1,0:T(1,128)} %param.9) | copy-start | bytes 98308
  4.8 61.7 %collective-permute-start.3 = (f32[1024,512]{1,0:T(8,128)}, f32[1024,512]{1,0:T(8,128)}, u32[]{:S(2)}, u32[]{:S(2)}) collective-permute-start(f32[1024,512]{1,0:T(8,128)} %get-tuple-element.17), channel_id=1, source_target_pairs={{0,1},{1,2},{2,3},{4,5},{5,6},{6,7},{8,9},{9,10},{10,11},{12,13},{... | collective-permute-start | bytes 6291464 | tf_op jit(solution)/shard_map/ppermute | solution.py:178
  10.0 90.2 %collective-permute-start = (f32[1024,512]{1,0:T(8,128)}, f32[1024,512]{1,0:T(8,128)}, u32[]{:S(2)}, u32[]{:S(2)}) collective-permute-start(f32[1024,512]{1,0:T(8,128)} %get-tuple-element.18), channel_id=1, source_target_pairs={{1,0},{2,1},{3,2},{5,4},{6,5},{7,6},{9,8},{10,9},{11,10},{13,12},{... | collective-permute-start | bytes 6291464 | tf_op jit(solution)/shard_map/ppermute | solution.py:178
  13.1 2.8 %copy-start.9 = (f32[1,8192]{1,0:T(1,128)S(1)}, f32[1,8192]{1,0:T(1,128)}, u32[]{:S(2)}) copy-start(f32[1,8192]{1,0:T(1,128)} %param.13) | copy-start | bytes 98308
  13.1 2.9 %copy-start.10 = (f32[1,8192]{1,0:T(1,128)S(1)}, f32[1,8192]{1,0:T(1,128)}, u32[]{:S(2)}) copy-start(f32[1,8192]{1,0:T(1,128)} %param.12) | copy-start | bytes 98308
  29.1 2.4 %copy-start.4 = (bf16[8,1280,256]{2,1,0:T(8,128)(2,1)}, bf16[8,1280,256]{2,1,0:T(8,128)(2,1)S(1)}, u32[]{:S(2)}) copy-start(bf16[8,1280,256]{2,1,0:T(8,128)(2,1)S(1)} %get-tuple-element.9) | copy-start | bytes 15728644
  29.1 4.1 %copy-start.2 = (bf16[8,1280,256]{2,1,0:T(8,128)(2,1)}, bf16[8,1280,256]{2,1,0:T(8,128)(2,1)S(1)}, u32[]{:S(2)}) copy-start(bf16[8,1280,256]{2,1,0:T(8,128)(2,1)S(1)} %get-tuple-element.10) | copy-start | bytes 15728644
  49.6 61.6 %collective-permute-start.7 = (f32[512,1024]{1,0:T(8,128)}, f32[512,1024]{1,0:T(8,128)S(1)}, u32[]{:S(2)}, u32[]{:S(2)}) collective-permute-start(f32[512,1024]{1,0:T(8,128)} %get-tuple-element.23), channel_id=1, source_target_pairs={{4,0},{8,4},{12,8},{16,12},{20,16},{24,20},{28,24},{5,1},{9,5},{13... | collective-permute-start | bytes 6291464 | tf_op jit(solution)/shard_map/ppermute | solution.py:178
  52.4 61.8 %collective-permute-start.6 = (f32[512,1024]{1,0:T(8,128)}, f32[512,1024]{1,0:T(8,128)}, u32[]{:S(2)}, u32[]{:S(2)}) collective-permute-start(f32[512,1024]{1,0:T(8,128)} %get-tuple-element.24), channel_id=1, source_target_pairs={{0,4},{4,8},{8,12},{12,16},{16,20},{20,24},{24,28},{1,5},{5,9},{9,... | collective-permute-start | bytes 6291464 | tf_op jit(solution)/shard_map/ppermute | solution.py:178
  55.7 8.4 %copy-start.3 = (bf16[8,1280,256]{2,1,0:T(8,128)(2,1)S(1)}, bf16[8,1280,256]{2,1,0:T(8,128)(2,1)}, u32[]{:S(2)}) copy-start(bf16[8,1280,256]{2,1,0:T(8,128)(2,1)} %copy-done.2) | copy-start | bytes 15728644
  64.2 1.5 %copy-start = (bf16[4,256,1280]{2,1,0:T(8,128)(2,1)}, bf16[4,256,1280]{2,1,0:T(8,128)(2,1)S(1)}, u32[]{:S(2)}) copy-start(bf16[4,256,1280]{2,1,0:T(8,128)(2,1)S(1)} %get-tuple-element.11.high_ref) | copy-start | bytes 7864324
  64.2 2.3 %copy-start.1 = (bf16[4,256,1280]{2,1,0:T(8,128)(2,1)}, bf16[4,256,1280]{2,1,0:T(8,128)(2,1)S(1)}, u32[]{:S(2)}) copy-start(bf16[4,256,1280]{2,1,0:T(8,128)(2,1)S(1)} %get-tuple-element.12.low_ref) | copy-start | bytes 7864324
  73.1 54.2 %collective-permute-start.5 = (f32[512,512]{1,0:T(8,128)S(1)}, f32[512,512]{1,0:T(8,128)S(1)}, u32[]{:S(2)}, u32[]{:S(2)}) collective-permute-start(f32[512,512]{1,0:T(8,128)S(1)} %get-tuple-element.25), channel_id=1, source_target_pairs={{4,0},{8,4},{12,8},{16,12},{20,16},{24,20},{28,24},{5,1},{9,5},{13... | collective-permute-start | bytes 3145736 | tf_op jit(solution)/shard_map/ppermute | solution.py:178
  75.4 51.9 %collective-permute-start.4 = (f32[512,512]{1,0:T(8,128)S(1)}, f32[512,512]{1,0:T(8,128)S(1)}, u32[]{:S(2)}, u32[]{:S(2)}) collective-permute-start(f32[512,512]{1,0:T(8,128)S(1)} %get-tuple-element.26), channel_id=1, source_target_pairs={{0,4},{4,8},{8,12},{12,16},{16,20},{20,24},{24,28},{1,5},{5,9},{9,... | collective-permute-start | bytes 3145736 | tf_op jit(solution)/shard_map/ppermute | solution.py:178
  107.7 27.8 %collective-permute-start.2 = (f32[512,512]{1,0:T(8,128)}, f32[512,512]{1,0:T(8,128)S(1)}, u32[]{:S(2)}, u32[]{:S(2)}) collective-permute-start(f32[512,512]{1,0:T(8,128)} %get-tuple-element.27), channel_id=1, source_target_pairs={{4,0},{8,4},{12,8},{16,12},{20,16},{24,20},{28,24},{5,1},{9,5},{13... | collective-permute-start | bytes 3145736 | tf_op jit(solution)/shard_map/ppermute | solution.py:178
  111.1 24.3 %collective-permute-start.1 = (f32[512,512]{1,0:T(8,128)S(1)}, f32[512,512]{1,0:T(8,128)S(1)}, u32[]{:S(2)}, u32[]{:S(2)}) collective-permute-start(f32[512,512]{1,0:T(8,128)S(1)} %get-tuple-element.28), channel_id=1, source_target_pairs={{0,4},{4,8},{8,12},{12,16},{16,20},{20,24},{24,28},{1,5},{5,9},{9,... | collective-permute-start | bytes 3145736 | tf_op jit(solution)/shard_map/ppermute | solution.py:178
